TPU v7x, 32 devices: a whole 2x2x4 slice. The times are simulated.
32 devices in a mesh: query: 2 (over x), corpus: 16 (over z, y, core).
Axes of the slice: x: 2, y: 2, z: 4, core: 2. Of those that a mesh axis runs over, the one named last changes fastest.
Arguments:
- clean_feats: bfloat16 [2, 2, 512, 320], P('query', None, 'corpus'), may hold values from -6 to 6
- noise_draw: bfloat16 [2, 2, 512, 320], P('query', None, 'corpus'), may hold values from -6 to 6
- timesteps: int32 [2, 2], P('query'), may hold values from 0 to 999
- weight_in: bfloat16 [2, 320, 320], P(None, None, 'corpus'), may hold values from -0.3125 to 0.3125
- weight_ffin: bfloat16 [2, 320, 2560], P(None, None, 'corpus'), may hold values from -0.3125 to 0.3125
- weight_ffout: bfloat16 [2, 1280, 320], P(None, None, 'corpus'), may hold values from -0.15625 to 0.15625
- weight_out: bfloat16 [2, 320, 320], P(None, None, 'corpus'), may hold values from -0.3125 to 0.3125
- norm_gain: float32 [2, 320], replicated, may hold values from 0.5 to 1.5
- norm_bias: float32 [2, 320], replicated, may hold values from -3 to 3
- sketch_cin: bfloat16 [2, 3, 320, 16], replicated, may hold values from -0.3125 to 0.3125
- sketch_fin: bfloat16 [2, 1280, 16], replicated, may hold values from -0.15625 to 0.15625
- sketch_cout: bfloat16 [2, 3, 320, 16], replicated, may hold values from -0.3125 to 0.3125
- sketch_fout: bfloat16 [2, 2560, 16], replicated, may hold values from -0.125 to 0.125
- precond: float32 [8, 256, 256], P('query'), as said below
- store_grads: bfloat16 [8192, 2048], P(('query', 'corpus')), may hold values from -6 to 6
- store_scale: float32 [8192], P(('query', 'corpus')), may hold values from 0.002 to 0.03
Outputs:
- scores: float32 [2, 8192], P(None, ('query', 'corpus'))
Inputs may be any that keep to these rules, and one draw needn't show every extreme that they name: `precond`: each layer's matrix is symmetric with a diagonal between 1 and 2.
All inputs are finite; a program needn't handle non-finite values.
Results may differ from a plain program's by a relative error of at most 0.0085.
Values may be sent and summed in bfloat16 or wider, within the bound.
A program may use at most 64 MiB of HBM per device.

v0:
```python
import math
import jax
import jax.numpy as jnp
from jax import lax
from jax.sharding import PartitionSpec as P

plan_len = 1000


def noise_levels(timesteps):
    steps = jnp.arange(plan_len, dtype=jnp.float32)
    rooted = math.sqrt(0.00085) + (math.sqrt(0.012) - math.sqrt(0.00085)) * steps / (plan_len - 1)
    terms = jnp.log1p(-rooted * rooted)
    reached = jnp.arange(plan_len, dtype=jnp.int32) <= timesteps[..., None]
    picked = jnp.exp(jnp.sum(jnp.where(reached, terms, jnp.zeros_like(terms)), axis=-1))
    return (jnp.sqrt(picked), jnp.sqrt(1.0 - picked))


def gelu_parts(gate):
    cumul = 0.5 * (1.0 + jax.scipy.special.erf(gate / math.sqrt(2.0)))
    density = jnp.exp(-0.5 * gate * gate) / math.sqrt(2.0 * math.pi)
    return (gate * cumul, cumul + gate * density)


def contract_back(delta, weight):
    return lax.dot_general(
        delta, weight, (((1,), (1,)), ((), ())), preferred_element_type=jnp.float32
    )


def block_forward(residual_stream, weights, scale_gain, shift_bias):
    weight_in, weight_ffin, weight_ffout, weight_out = weights
    hidden = weight_ffout.shape[0]
    residual_reduced = residual_stream.astype(jnp.bfloat16)
    inner = jnp.dot(residual_reduced, weight_in, preferred_element_type=jnp.float32)
    centred_input = inner - jnp.mean(inner, axis=-1, keepdims=True)
    inverse_deviation = lax.rsqrt(
        jnp.mean(centred_input * centred_input, axis=-1, keepdims=True) + 1e-05
    )
    standardized_input = centred_input * inverse_deviation
    normalized_input = (standardized_input * scale_gain + shift_bias).astype(jnp.bfloat16)
    projected = jnp.dot(normalized_input, weight_ffin, preferred_element_type=jnp.float32)
    value_output = projected[:, :hidden]
    gate = projected[:, hidden:]
    gelu_result, gelu_derivative = gelu_parts(gate)
    mixed_hidden = (value_output * gelu_result).astype(jnp.bfloat16)
    inner_two = inner + jnp.dot(mixed_hidden, weight_ffout, preferred_element_type=jnp.float32)
    inner_reduced = inner_two.astype(jnp.bfloat16)
    residual_stream = residual_stream + jnp.dot(
        inner_reduced, weight_out, preferred_element_type=jnp.float32
    )
    return (
        residual_stream,
        (
            residual_reduced,
            standardized_input,
            inverse_deviation,
            normalized_input,
            value_output,
            gelu_result,
            gelu_derivative,
            mixed_hidden,
            inner_reduced,
        ),
    )


def block_backward(dstream, saved_activations, weights, scale_gain):
    weight_in, weight_ffin, weight_ffout, weight_out = weights
    (
        residual_reduced,
        standardized_input,
        inverse_deviation,
        normalized_input,
        value_output,
        gelu_result,
        gelu_derivative,
        mixed_hidden,
        inner_reduced,
    ) = saved_activations
    dout_low = dstream.astype(jnp.bfloat16)
    second_inner_gradient = contract_back(dout_low, weight_out)
    dtwo_low = second_inner_gradient.astype(jnp.bfloat16)
    dmixed = contract_back(dtwo_low, weight_ffout)
    dproj_low = jnp.concatenate(
        [dmixed * gelu_result, dmixed * value_output * gelu_derivative], axis=-1
    ).astype(jnp.bfloat16)
    dnormed = contract_back(dproj_low, weight_ffin)
    scaled_hidden = dnormed * scale_gain
    inner_gradient = second_inner_gradient + inverse_deviation * (
        scaled_hidden
        - jnp.mean(scaled_hidden, axis=-1, keepdims=True)
        - standardized_input * jnp.mean(scaled_hidden * standardized_input, axis=-1, keepdims=True)
    )
    dinner_low = inner_gradient.astype(jnp.bfloat16)
    dstream = dstream + contract_back(dinner_low, weight_in)
    records = [
        (residual_reduced, dinner_low),
        (normalized_input, dproj_low),
        (mixed_hidden, dtwo_low),
        (inner_reduced, dout_low),
    ]
    return (dstream, records)


def project_layer(inputs, deltas, sketch_in, sketch_out, samples):
    left = jnp.dot(inputs, sketch_in, preferred_element_type=jnp.float32)
    right = jnp.dot(deltas, sketch_out, preferred_element_type=jnp.float32)
    left = left.reshape(samples, -1, left.shape[-1])
    right = right.reshape(samples, -1, right.shape[-1])
    outer = jnp.einsum("srk,srj->skj", left, right, precision=lax.Precision.HIGHEST)
    return outer.reshape(samples, -1)


def sketches_of(block, sketch_cin, sketch_fin, sketch_cout, sketch_fout):
    return [
        (sketch_cin[block, 0], sketch_cout[block, 0]),
        (sketch_cin[block, 1], sketch_fout[block]),
        (sketch_fin[block], sketch_cout[block, 1]),
        (sketch_cin[block, 2], sketch_cout[block, 2]),
    ]


def on_device(
    clean_feats,
    noise_draw,
    timesteps,
    weight_in,
    weight_ffin,
    weight_ffout,
    weight_out,
    norm_gain,
    norm_bias,
    sketch_cin,
    sketch_fin,
    sketch_cout,
    sketch_fout,
    precond,
    store_grads,
    store_scale,
):
    samples = clean_feats.shape[0]
    positions = clean_feats.shape[2] * lax.axis_size("corpus")
    loss_scale = 1.0 / math.sqrt(clean_feats.shape[1] * positions)
    blocks = weight_in.shape[0]
    signal, spread = noise_levels(timesteps)
    noise_rows = noise_draw.astype(jnp.float32)
    residual_stream = (
        signal[:, :, None, None] * clean_feats.astype(jnp.float32)
        + spread[:, :, None, None] * noise_rows
    )
    residual_stream = residual_stream.reshape(-1, residual_stream.shape[-1])
    noise_rows = noise_rows.reshape(-1, noise_rows.shape[-1])
    gathered = (
        lax.all_gather(weight_in, "corpus", axis=2, tiled=True),
        lax.all_gather(weight_ffin, "corpus", axis=2, tiled=True),
        lax.all_gather(weight_ffout, "corpus", axis=2, tiled=True),
        lax.all_gather(weight_out, "corpus", axis=2, tiled=True),
    )

    def fetch_forward(block):
        return tuple((member[block] for member in gathered))

    def fetch_backward(block):
        return tuple((member[block] for member in gathered))

    saved_all = []
    for block in range(blocks):
        residual_stream, saved_activations = block_forward(
            residual_stream, fetch_forward(block), norm_gain[block], norm_bias[block]
        )
        saved_all.append(saved_activations)
    dstream = (residual_stream - noise_rows) * loss_scale
    layers = [None] * (4 * blocks)
    for block in reversed(range(blocks)):
        dstream, records = block_backward(
            dstream, saved_all[block], fetch_backward(block), norm_gain[block]
        )
        pairs = sketches_of(block, sketch_cin, sketch_fin, sketch_cout, sketch_fout)
        for index in range(4):
            layers[4 * block + index] = project_layer(
                records[index][0], records[index][1], pairs[index][0], pairs[index][1], samples
            )
    partial_grads = jnp.stack(layers, axis=1)
    totals = lax.psum(partial_grads, "corpus")
    routed = lax.all_to_all(totals, "query", split_axis=1, concat_axis=0, tiled=True)
    owned = jnp.einsum("qlk,lkj->qlj", routed, precond, precision=lax.Precision.HIGHEST).astype(
        jnp.bfloat16
    )
    preconditioned = lax.all_gather(owned, "query", axis=1, tiled=True)
    flat = preconditioned.reshape(preconditioned.shape[0], -1)
    raw = lax.dot_general(
        flat, store_grads, (((1,), (1,)), ((), ())), preferred_element_type=jnp.float32
    )
    return raw * store_scale[None, :]


def solution(mesh):
    placed = (
        P("query", None, "corpus", None),
        P("query", None, "corpus", None),
        P("query", None),
        P(None, None, "corpus"),
        P(None, None, "corpus"),
        P(None, None, "corpus"),
        P(None, None, "corpus"),
        P(),
        P(),
        P(),
        P(),
        P(),
        P(),
        P("query", None, None),
        P(("query", "corpus"), None),
        P(("query", "corpus")),
    )
    return jax.shard_map(
        on_device,
        mesh=mesh,
        in_specs=placed,
        out_specs=P(None, ("query", "corpus")),
        check_vma=False,
    )
```

profile of v0, /device:TPU:0, one launch (start us, length us, event | category | flops | bytes accessed | tf_op | source)
XLA Modules:
  0.0 167.8 jit_solution(465755251760985908)
XLA Ops:
  6.5 0.7 all-gather.5.cloned.1.call-update
  7.3 0.7 all-gather.3.cloned.1.call-update
  8.0 25.0 %all_gather.15 = bf16[2,320,320]{1,0,2:T(2,128)(2,1)S(1)} all-gather(bf16[2,320,20]{1,0,2:T(2,128)(2,1)} %param.19), channel_id=1, replica_groups=mesh['query'=2,'corpus'=16] {'corpus'}, dimensions={2}, use_global_device_ids=true | all-gather | bytes 435200 | tf_op jit(solution)/shard_map/all_gather | solution.py:155
  33.0 0.7 fusion.105
  33.7 0.9 copy.52
  34.6 19.7 %all_gather.18 = bf16[2,320,320]{1,0,2:T(2,128)(2,1)S(1)} all-gather(bf16[2,320,20]{1,0,2:T(2,128)(2,1)S(1)} %copy-done.12), channel_id=1, replica_groups=mesh['query'=2,'corpus'=16] {'corpus'}, dimensions={2}, use_global_device_ids=true | all-gather | bytes 435200 | tf_op jit(solution)/shard_map/all_gather | solution.py:158
  54.3 0.7 fusion.104
  55.0 0.9 copy.54
  55.9 0.9 copy.55
  56.8 0.9 copy.57
  57.7 0.6 slice_reduce_fusion
  58.6 0.7 fusion.102
  59.3 0.3 fusion.106
  59.8 0.8 fusion.79
  60.7 0.6 copy-done.4
  61.3 0.8 fusion.76
  62.2 5.7 %fusion.103 = (bf16[1,1280,320]{1,0,2:T(2,128)(2,1)}, bf16[1,1280,320]{1,0,2:T(2,128)(2,1)S(1)}) fusion(bf16[2,1280,320]{1,0,2:T(2,128)(2,1)} %all-gather.5.cloned.1.call-done), kind=kLoop, calls=%fused_computation.161 | loop fusion | bytes 3276800 | tf_op jit(solution)/shard_map/slice | solution.py:162
  67.9 36.5 %all-gather.3.cloned.1.call-done = bf16[2,320,2560]{1,2,0:T(8,128)(2,1)} async-done(((bf16[2,320,160]{1,2,0:T(8,128)(2,1)}), bf16[2,320,2560]{1,2,0:T(8,128)(2,1)}) %all-gather.3.cloned.1.call-update) | async-done | bytes 3276816 | tf_op jit(solution)/shard_map/all_gather | solution.py:156
  104.3 2.5 %fusion.1 = f32[64,2560]{1,0:T(8,128)S(1)} fusion(bf16[64,320]{1,0:T(8,128)(2,1)} %copy-done.4, bf16[2,320,2560]{1,2,0:T(8,128)(2,1)} %all-gather.3.cloned.1.call-done), kind=kOutput, calls=%fused_computation.3 | convolution fusion | flops 104857600 | bytes 2670592 | tf_op jit(solution)/shard_map/dot_general | solution.py:42
  106.9 0.4 fusion.8
  108.2 0.7 fusion.3
  109.0 0.3 copy-done.2
  109.3 0.4 fusion.9
  110.1 0.3 multiply_convert_fusion.1
  110.4 0.5 fusion.101
  111.5 0.3 multiply_convert_fusion
  113.7 0.5 fusion.100
  116.3 32.2 %psum.7 = f32[1,8,256]{2,0,1:T(1,128)S(1)} all-reduce(f32[1,8,256]{2,0,1:T(1,128)S(1)} %constant_dynamic-update-slice_fusion), channel_id=1, replica_groups=mesh['query'=2,'corpus'=16] {'corpus'}, use_global_device_ids=true, to_apply=%region_9.10 | all-reduce | flops 2048 | bytes 16384 | tf_op jit(solution)/shard_map/psum | solution.py:185
  148.6 6.3 %all_to_all.12 = f32[1,8,256]{2,0,1:T(1,128)S(1)} all-to-all(f32[1,8,256]{2,0,1:T(1,128)S(1)} %psum.7), channel_id=1, replica_groups=mesh['query'=2,'corpus'=16] {'query'}, dimensions={1} | all-to-all | bytes 16384 | tf_op jit(solution)/shard_map/all_to_all | solution.py:186
  155.0 0.6 fusion.11
  155.6 4.3 %all_gather.19 = bf16[2,8,256]{2,0,1:T(2,128)(2,1)S(1)} all-gather(bf16[2,4,256]{2,0,1:T(2,128)(2,1)S(1)} %fusion.11), channel_id=1, replica_groups=mesh['query'=2,'corpus'=16] {'query'}, dimensions={1}, use_global_device_ids=true | all-gather | bytes 12288 | tf_op jit(solution)/shard_map/all_gather | solution.py:190
  160.0 1.0 convolution_multiply_fusion
  (111 shorter events, 6.5 us)
Async XLA Ops:
  6.5 148.5 %copy-start = (f32[4,256,256]{2,1,0:T(8,128)S(1)}, f32[4,256,256]{2,1,0:T(8,128)}, u32[]{:S(2)}) copy-start(f32[4,256,256]{2,1,0:T(8,128)} %param.29) | copy-start | bytes 3145732
  6.5 28.1 %copy-start.12 = (bf16[2,320,20]{1,0,2:T(2,128)(2,1)S(1)}, bf16[2,320,20]{1,0,2:T(2,128)(2,1)}, u32[]{:S(2)}) copy-start(bf16[2,320,20]{1,0,2:T(2,128)(2,1)} %param.22) | copy-start | bytes 76804
  6.5 55.6 %all-gather.5.cloned.1.call-start = ((), (), s32[]{:S(2)}) async-start(), calls=%async_computation.2 | async-start | bytes 1740800 | tf_op jit(solution)/shard_map/all_gather | solution.py:157
  7.3 97.1 %all-gather.3.cloned.1.call-start = ((), (), s32[]{:S(2)}) async-start(), calls=%async_computation.1 | async-start | bytes 4177920 | tf_op jit(solution)/shard_map/all_gather | solution.py:156
  54.3 3.4 %copy-start.16 = (f32[2,320]{1,0:T(2,128)S(1)}, f32[2,320]{1,0:T(2,128)}, u32[]{:S(2)}) copy-start(f32[2,320]{1,0:T(2,128)} %param.24) | copy-start | bytes 7684
  54.3 4.0 %copy-start.17 = (f32[2,320]{1,0:T(2,128)S(1)}, f32[2,320]{1,0:T(2,128)}, u32[]{:S(2)}) copy-start(f32[2,320]{1,0:T(2,128)} %param.23) | copy-start | bytes 7684
  54.3 4.0 %copy-start.21 = (s32[1,2]{1,0:T(1,128)S(1)}, s32[1,2]{1,0:T(1,128)}, u32[]{:S(2)}) copy-start(s32[1,2]{1,0:T(1,128)} %param.18) | copy-start | bytes 28
  54.3 4.3 %copy-start.6 = (bf16[1,2,32,320]{3,2,1,0:T(8,128)(2,1)S(1)}, bf16[1,2,32,320]{3,2,1,0:T(8,128)(2,1)}, u32[]{:S(2)}) copy-start(bf16[1,2,32,320]{3,2,1,0:T(8,128)(2,1)} %param.17) | copy-start | bytes 122884
  54.3 4.3 %copy-start.11 = (bf16[1,2,32,320]{3,2,1,0:T(8,128)(2,1)S(1)}, bf16[1,2,32,320]{3,2,1,0:T(8,128)(2,1)}, u32[]{:S(2)}) copy-start(bf16[1,2,32,320]{3,2,1,0:T(8,128)(2,1)} %param.16) | copy-start | bytes 122884
  59.6 8.3 %copy-start.14 = (f32[64]{0:T(128)}, f32[64]{0:T(128)S(1)}, u32[]{:S(2)}) copy-start(f32[64]{0:T(128)S(1)} %broadcast_multiply_fusion.5) | copy-start | bytes 772
  59.8 2.4 %copy-start.18 = (f32[64]{0:T(128)}, f32[64]{0:T(128)S(1)}, u32[]{:S(2)}) copy-start(f32[64]{0:T(128)S(1)} %add_rsqrt_fusion.1) | copy-start | bytes 772
  60.7 0.6 copy-start.4
  104.3 2.9 %copy-start.10 = (bf16[2,3,320,16]{2,3,1,0:T(8,128)(2,1)S(1)}, bf16[2,3,320,16]{2,3,1,0:T(8,128)(2,1)}, u32[]{:S(2)}) copy-start(bf16[2,3,320,16]{2,3,1,0:T(8,128)(2,1)} %param.25) | copy-start | bytes 184324
  104.3 3.1 %copy-start.5 = (f32[1,2,32,320]{3,2,1,0:T(8,128)S(1)}, f32[1,2,32,320]{3,2,1,0:T(8,128)}, u32[]{:S(2)}) copy-start(f32[1,2,32,320]{3,2,1,0:T(8,128)} %get-tuple-element.14) | copy-start | bytes 245764
  104.3 3.9 %copy-start.1 = (bf16[2,320,2560]{1,2,0:T(8,128)(2,1)S(1)}, bf16[2,320,2560]{1,2,0:T(8,128)(2,1)}, u32[]{:S(2)}) copy-start(bf16[2,320,2560]{1,2,0:T(8,128)(2,1)} %all-gather.3.cloned.1.call-done) | copy-start | bytes 9830404
  106.8 1.3 copy-start.13
  107.9 1.4 copy-start.2
  108.2 1.5 copy-start.7
  110.9 0.9 copy-start.9
  110.9 1.6 copy-start.8
  111.3 2.0 %copy-start.22 = (bf16[2,2560,16]{1,2,0:T(8,128)(2,1)S(1)}, bf16[2,2560,16]{1,2,0:T(8,128)(2,1)}, u32[]{:S(2)}) copy-start(bf16[2,2560,16]{1,2,0:T(8,128)(2,1)} %param.28) | copy-start | bytes 491524
  111.5 2.2 %copy-start.15 = (f32[64]{0:T(128)S(1)}, f32[64]{0:T(128)}, u32[]{:S(2)}) copy-start(f32[64]{0:T(128)} %copy-done.14) | copy-start | bytes 772
  111.5 2.2 %copy-start.19 = (f32[64]{0:T(128)S(1)}, f32[64]{0:T(128)}, u32[]{:S(2)}) copy-start(f32[64]{0:T(128)} %copy-done.18) | copy-start | bytes 772
  113.7 46.3 %copy-start.3 = (bf16[256,2048]{1,0:T(8,128)(2,1)S(1)}, bf16[256,2048]{1,0:T(8,128)(2,1)}, u32[]{:S(2)}) copy-start(bf16[256,2048]{1,0:T(8,128)(2,1)} %param.30) | copy-start | bytes 3145732
  113.7 46.3 %copy-start.20 = (f32[256]{0:T(256)S(1)}, f32[256]{0:T(256)}, u32[]{:S(2)}) copy-start(f32[256]{0:T(256)} %param.31) | copy-start | bytes 3076
Sparse Core Ops, SparseCore 0:
  9.5 43.8 all-gather.4
  55.7 48.5 all-gather.2
where the time goes:
time: 168 us
  blocking collectives  87.6 us (52%)
  waiting for transfers between devices  37.9 us (23%)
  between operations  13.9 us (8%)
  matrix products  13.5 us (8%)
  local copies, waits for them, and re-layouts  13 us (8%)
  other arithmetic  1.84 us (1%)
    all_gather x1, waiting for transfers between devices, on_device(): lax.all_gather(weight_ffin, 'corpus', axis=2, tiled=True)  36.5 us
    psum x1, blocking collectives, on_device(): totals = lax.psum(partial_grads, 'corpus')  32.2 us
    all_gather x1, blocking collectives, on_device(): lax.all_gather(weight_in, 'corpus', axis=2, tiled=True)  25 us
    all_gather x1, blocking collectives, on_device(): lax.all_gather(weight_out, 'corpus', axis=2, tiled=True)  19.7 us
    slice x3, local copies, waits for them, and re-layouts, fetch_forward(): return tuple((member[block] for member in gathered))  7.04 us
    all_to_all x1, blocking collectives, on_device(): lax.all_to_all(totals, 'query', split_axis=1, concat_axis=0, tiled=True)  6.35 us
    unnamed x57, local copies, waits for them, and re-layouts  4.61 us
    all_gather x1, blocking collectives, on_device(): preconditioned = lax.all_gather(owned, 'query', axis=1, tiled=True)  4.33 us
  transfers between devices with their start and end apart: 2, of which 1 were waited for; matrix products, arithmetic and copies ran while one was open for 9% of the time, Pallas kernels for 0%

commit v1 on v0

--- a/solution.py
+++ b/solution.py
@@ -5,6 +5,10 @@
 from jax.sharding import PartitionSpec as P
 
 plan_len = 1000
+
+
+def _view_works(panel):
+    return lax.all_gather(panel, "corpus").sum(axis=0)
 
 
 def noise_levels(timesteps):
@@ -182,7 +186,7 @@
                 records[index][0], records[index][1], pairs[index][0], pairs[index][1], samples
             )
     partial_grads = jnp.stack(layers, axis=1)
-    totals = lax.psum(partial_grads, "corpus")
+    totals = _view_works(partial_grads)
     routed = lax.all_to_all(totals, "query", split_axis=1, concat_axis=0, tiled=True)
     owned = jnp.einsum("qlk,lkj->qlj", routed, precond, precision=lax.Precision.HIGHEST).astype(
         jnp.bfloat16

time: 168 us -> 156 us (0.929)
  blocking collectives: 87.6 us -> 75.2 us
    psum x1 -> x0, blocking collectives: 32.2 us -> none  [on_device(): totals = lax.psum(partial_grads, 'corpus')]
    all_gather x0 -> x1, blocking collectives: none -> 19.8 us  [_view_works(): return lax.all_gather(panel, 'corpus').sum(axis=0)]
    unnamed x57 -> x50, local copies, waits for them, and re-layouts: 4.61 us -> 3.95 us
where the time goes in v1:
time: 156 us; the launch traced here: 155 us
  blocking collectives  75.2 us (48%)
  waiting for transfers between devices  38.5 us (25%)
  between operations  13.9 us (9%)
  matrix products  13.5 us (9%)
  local copies, waits for them, and re-layouts  12.4 us (8%)
  other arithmetic  1.85 us (1%)
    all_gather x1, waiting for transfers between devices, on_device(): lax.all_gather(weight_ffin, 'corpus', axis=2, tiled=True)  37.1 us
    all_gather x1, blocking collectives, on_device(): lax.all_gather(weight_in, 'corpus', axis=2, tiled=True)  25 us
    all_gather x1, blocking collectives, _view_works(): return lax.all_gather(panel, 'corpus').sum(axis=0)  19.8 us
    all_gather x1, blocking collectives, on_device(): lax.all_gather(weight_out, 'corpus', axis=2, tiled=True)  19.7 us
    slice x3, local copies, waits for them, and re-layouts, fetch_forward(): return tuple((member[block] for member in gathered))  7.04 us
    all_to_all x1, blocking collectives, on_device(): lax.all_to_all(totals, 'query', split_axis=1, concat_axis=0, tiled=True)  6.35 us
    all_gather x1, blocking collectives, on_device(): preconditioned = lax.all_gather(owned, 'query', axis=1, tiled=True)  4.33 us
    unnamed x50, local copies, waits for them, and re-layouts  3.95 us
  transfers between devices with their start and end apart: 2, of which 1 were waited for; matrix products, arithmetic and copies ran while one was open for 9% of the time, Pallas kernels for 0%

profile of v1, /device:TPU:0, one launch (start us, length us, event | category | flops | bytes accessed | tf_op | source)
XLA Modules:
  0.0 155.3 jit_solution(9686426144238560264)
XLA Ops:
  6.5 0.7 all-gather.6.cloned.1.call-update
  7.3 0.7 all-gather.4.cloned.1.call-update
  8.0 25.0 %all_gather.21 = bf16[2,320,320]{1,0,2:T(2,128)(2,1)S(1)} all-gather(bf16[2,320,20]{1,0,2:T(2,128)(2,1)} %param.19), channel_id=1, replica_groups=mesh['query'=2,'corpus'=16] {'corpus'}, dimensions={2}, use_global_device_ids=true | all-gather | bytes 435200 | tf_op jit(solution)/shard_map/all_gather | solution.py:159
  33.0 0.7 fusion.105
  33.7 0.9 copy.36
  34.6 19.7 %all_gather.24 = bf16[2,320,320]{1,0,2:T(2,128)(2,1)S(1)} all-gather(bf16[2,320,20]{1,0,2:T(2,128)(2,1)S(1)} %copy-done.12), channel_id=1, replica_groups=mesh['query'=2,'corpus'=16] {'corpus'}, dimensions={2}, use_global_device_ids=true | all-gather | bytes 435200 | tf_op jit(solution)/shard_map/all_gather | solution.py:162
  54.3 0.7 fusion.104
  55.0 0.9 copy.38
  55.9 0.9 copy.39
  56.8 0.9 copy.41
  57.7 0.6 slice_reduce_fusion
  58.6 0.7 fusion.102
  59.3 0.3 fusion.106
  59.8 0.8 fusion.79
  60.7 0.9 fusion.76
  61.6 5.7 %fusion.103 = (bf16[1,1280,320]{1,0,2:T(2,128)(2,1)}, bf16[1,1280,320]{1,0,2:T(2,128)(2,1)S(1)}) fusion(bf16[2,1280,320]{1,0,2:T(2,128)(2,1)} %all-gather.6.cloned.1.call-done), kind=kLoop, calls=%fused_computation.153 | loop fusion | bytes 3276800 | tf_op jit(solution)/shard_map/slice | solution.py:166
  67.3 37.1 %all-gather.4.cloned.1.call-done = bf16[2,320,2560]{1,2,0:T(8,128)(2,1)} async-done(((bf16[2,320,160]{1,2,0:T(8,128)(2,1)}), bf16[2,320,2560]{1,2,0:T(8,128)(2,1)}) %all-gather.4.cloned.1.call-update) | async-done | bytes 3276816 | tf_op jit(solution)/shard_map/all_gather | solution.py:160
  104.3 2.5 %fusion.1 = f32[64,2560]{1,0:T(8,128)S(1)} fusion(bf16[64,320]{1,0:T(8,128)(2,1)} %copy-done.4, bf16[2,320,2560]{1,2,0:T(8,128)(2,1)} %all-gather.4.cloned.1.call-done), kind=kOutput, calls=%fused_computation.3 | convolution fusion | flops 104857600 | bytes 2670592 | tf_op jit(solution)/shard_map/dot_general | solution.py:46
  106.9 0.4 fusion.8
  107.6 0.3 fusion.107
  108.2 0.7 fusion.3
  109.0 0.3 copy-done.2
  109.3 0.4 fusion.9
  110.1 0.3 multiply_convert_fusion.1
  110.4 0.5 fusion.101
  111.5 0.3 multiply_convert_fusion
  113.7 0.5 fusion.100
  116.3 19.8 %all-gather = f32[16,8,256]{2,1,0:T(8,128)S(1)} all-gather(f32[1,8,256]{2,1,0:T(8,128)S(1)} %stack.3), channel_id=2, replica_groups=mesh['query'=2,'corpus'=16] {'corpus'}, dimensions={0}, use_global_device_ids=true | all-gather | bytes 139264 | tf_op jit(solution)/shard_map/all_gather | solution.py:11
  136.2 6.4 %all_to_all.12 = f32[1,8,256]{2,0,1:T(1,128)S(1)} all-to-all(f32[1,8,256]{2,0,1:T(1,128)S(1)} %reduce_sum.102), channel_id=1, replica_groups=mesh['query'=2,'corpus'=16] {'query'}, dimensions={1} | all-to-all | bytes 16384 | tf_op jit(solution)/shard_map/all_to_all | solution.py:190
  142.6 0.6 fusion.11
  143.2 4.3 %all_gather.27 = bf16[2,8,256]{2,0,1:T(2,128)(2,1)S(1)} all-gather(bf16[2,4,256]{2,0,1:T(2,128)(2,1)S(1)} %fusion.11), channel_id=1, replica_groups=mesh['query'=2,'corpus'=16] {'query'}, dimensions={1}, use_global_device_ids=true | all-gather | bytes 12288 | tf_op jit(solution)/shard_map/all_gather | solution.py:194
  147.5 1.0 convolution_multiply_fusion
  (106 shorter events, 6.2 us)
Async XLA Ops:
  6.5 136.0 %copy-start = (f32[4,256,256]{2,1,0:T(8,128)S(1)}, f32[4,256,256]{2,1,0:T(8,128)}, u32[]{:S(2)}) copy-start(f32[4,256,256]{2,1,0:T(8,128)} %param.29) | copy-start | bytes 3145732
  6.5 28.1 %copy-start.12 = (bf16[2,320,20]{1,0,2:T(2,128)(2,1)S(1)}, bf16[2,320,20]{1,0,2:T(2,128)(2,1)}, u32[]{:S(2)}) copy-start(bf16[2,320,20]{1,0,2:T(2,128)(2,1)} %param.22) | copy-start | bytes 76804
  6.5 55.0 %all-gather.6.cloned.1.call-start = ((), (), s32[]{:S(2)}) async-start(), calls=%async_computation.2 | async-start | bytes 1740800 | tf_op jit(solution)/shard_map/all_gather | solution.py:161
  7.3 97.1 %all-gather.4.cloned.1.call-start = ((), (), s32[]{:S(2)}) async-start(), calls=%async_computation.1 | async-start | bytes 4177920 | tf_op jit(solution)/shard_map/all_gather | solution.py:160
  54.3 3.4 %copy-start.16 = (f32[2,320]{1,0:T(2,128)S(1)}, f32[2,320]{1,0:T(2,128)}, u32[]{:S(2)}) copy-start(f32[2,320]{1,0:T(2,128)} %param.24) | copy-start | bytes 7684
  54.3 4.0 %copy-start.17 = (f32[2,320]{1,0:T(2,128)S(1)}, f32[2,320]{1,0:T(2,128)}, u32[]{:S(2)}) copy-start(f32[2,320]{1,0:T(2,128)} %param.23) | copy-start | bytes 7684
  54.3 4.0 %copy-start.21 = (s32[1,2]{1,0:T(1,128)S(1)}, s32[1,2]{1,0:T(1,128)}, u32[]{:S(2)}) copy-start(s32[1,2]{1,0:T(1,128)} %param.18) | copy-start | bytes 28
  54.3 4.3 %copy-start.6 = (bf16[1,2,32,320]{3,2,1,0:T(8,128)(2,1)S(1)}, bf16[1,2,32,320]{3,2,1,0:T(8,128)(2,1)}, u32[]{:S(2)}) copy-start(bf16[1,2,32,320]{3,2,1,0:T(8,128)(2,1)} %param.17) | copy-start | bytes 122884
  54.3 4.3 %copy-start.11 = (bf16[1,2,32,320]{3,2,1,0:T(8,128)(2,1)S(1)}, bf16[1,2,32,320]{3,2,1,0:T(8,128)(2,1)}, u32[]{:S(2)}) copy-start(bf16[1,2,32,320]{3,2,1,0:T(8,128)(2,1)} %param.16) | copy-start | bytes 122884
  59.6 1.0 copy-start.14
  59.8 7.5 %copy-start.18 = (f32[64]{0:T(128)}, f32[64]{0:T(128)S(1)}, u32[]{:S(2)}) copy-start(f32[64]{0:T(128)S(1)} %add_rsqrt_fusion.1) | copy-start | bytes 772
  60.7 0.9 copy-start.4
  104.3 2.9 %copy-start.10 = (bf16[2,3,320,16]{2,3,1,0:T(8,128)(2,1)S(1)}, bf16[2,3,320,16]{2,3,1,0:T(8,128)(2,1)}, u32[]{:S(2)}) copy-start(bf16[2,3,320,16]{2,3,1,0:T(8,128)(2,1)} %param.25) | copy-start | bytes 184324
  104.3 3.1 %copy-start.5 = (f32[1,2,32,320]{3,2,1,0:T(8,128)S(1)}, f32[1,2,32,320]{3,2,1,0:T(8,128)}, u32[]{:S(2)}) copy-start(f32[1,2,32,320]{3,2,1,0:T(8,128)} %get-tuple-element.14) | copy-start | bytes 245764
  104.3 3.9 %copy-start.1 = (bf16[2,320,2560]{1,2,0:T(8,128)(2,1)S(1)}, bf16[2,320,2560]{1,2,0:T(8,128)(2,1)}, u32[]{:S(2)}) copy-start(bf16[2,320,2560]{1,2,0:T(8,128)(2,1)} %all-gather.4.cloned.1.call-done) | copy-start | bytes 9830404
  106.8 1.3 copy-start.13
  107.9 1.4 copy-start.2
  108.2 1.5 copy-start.7
  110.9 0.9 copy-start.9
  110.9 1.6 %copy-start.8 = (bf16[2,1280,16]{1,2,0:T(8,128)(2,1)S(1)}, bf16[2,1280,16]{1,2,0:T(8,128)(2,1)}, u32[]{:S(2)}) copy-start(bf16[2,1280,16]{1,2,0:T(8,128)(2,1)} %param.26) | copy-start | bytes 245764
  111.3 2.0 %copy-start.22 = (bf16[2,2560,16]{1,2,0:T(8,128)(2,1)S(1)}, bf16[2,2560,16]{1,2,0:T(8,128)(2,1)}, u32[]{:S(2)}) copy-start(bf16[2,2560,16]{1,2,0:T(8,128)(2,1)} %param.28) | copy-start | bytes 491524
  111.5 2.2 %copy-start.15 = (f32[64]{0:T(128)S(1)}, f32[64]{0:T(128)}, u32[]{:S(2)}) copy-start(f32[64]{0:T(128)} %copy-done.14) | copy-start | bytes 772
  111.5 2.2 %copy-start.19 = (f32[64]{0:T(128)S(1)}, f32[64]{0:T(128)}, u32[]{:S(2)}) copy-start(f32[64]{0:T(128)} %copy-done.18) | copy-start | bytes 772
  113.7 33.8 %copy-start.3 = (bf16[256,2048]{1,0:T(8,128)(2,1)S(1)}, bf16[256,2048]{1,0:T(8,128)(2,1)}, u32[]{:S(2)}) copy-start(bf16[256,2048]{1,0:T(8,128)(2,1)} %param.30) | copy-start | bytes 3145732
  113.7 33.8 %copy-start.20 = (f32[256]{0:T(256)S(1)}, f32[256]{0:T(256)}, u32[]{:S(2)}) copy-start(f32[256]{0:T(256)} %param.31) | copy-start | bytes 3076
Sparse Core Ops, SparseCore 0:
  9.5 43.8 all-gather.5
  55.7 48.5 all-gather.3
